TPU v7x, 256 devices: a whole 4x4x8 slice. The times are simulated.
256 devices in a mesh: ctx: 256 (over y, z, x, core).
Axes of the slice: x: 4, y: 4, z: 8, core: 2. Of those that a mesh axis runs over, the one named last changes fastest.
Arguments:
- queries: bfloat16 [131072, 2048], P('ctx'), may hold values from -26 to 26
- attention_key_rows: bfloat16 [131072, 256], P('ctx'), may hold values from -4 to 4
- attention_value_rows: bfloat16 [131072, 256], P('ctx'), may hold values from -6 to 6
- output_gradient: bfloat16 [131072, 2048], P('ctx'), may hold values from -6 to 6
- parent_block: int32 [1024], replicated, may hold values from -1 to 1022, as said below
- seg_start: int32 [1024], replicated, may hold values from 0 to 127
Outputs:
- grad_queries: bfloat16 [131072, 2048], P('ctx')
- key_gradient_rows: bfloat16 [131072, 256], P('ctx')
- value_gradient_rows: bfloat16 [131072, 256], P('ctx')
Inputs may be any that keep to these rules, and one draw needn't show every extreme that they name: parent_block[g] is -1 or an earlier block lying on the same shard or on one of the 3 shards before it: parent_block[g] // 4 >= g // 4 - 3; that farthest distance is used in every draw.
All inputs are finite; a program needn't handle non-finite values.
Results may differ from a plain program's by a relative error of at most 0.007.
Values may be sent and summed in bfloat16 or wider, within the bound.
A program may use at most 64 MiB of HBM per device.

v0:
```python
import jax
import jax.numpy as jnp
from jax import lax
from jax.sharding import PartitionSpec as P

QUERY_HEADS = 32
KEY_VALUE_HEADS = 4
HEAD_SIZE = 64
BLOCK_TOKENS = 128
PARENT_SHARDS = 4


NEG_FILL = -1e30


def from_behind(value, axis, steps):
    count = lax.axis_size(axis)
    first, last = (max(0, -steps), min(count, count - steps))
    return lax.ppermute(value, axis, [(source, source + steps) for source in range(first, last)])


def block_masks(parent_here, start_here, start_parent):
    query_pos = jnp.arange(BLOCK_TOKENS)[None, :, None]
    key_pos = jnp.arange(BLOCK_TOKENS)[None, None, :]
    seg_own = start_here[:, None, None]
    seg_far = start_parent[:, None, None]
    own_keys = (key_pos <= query_pos) & ((key_pos >= seg_own) == (query_pos >= seg_own))
    carried = (query_pos < seg_own) | (seg_own == 0)
    far_keys = (
        (parent_here[:, None, None] >= 0) & carried & (key_pos > query_pos) & (key_pos >= seg_far)
    )
    return jnp.concatenate([far_keys, own_keys], axis=2)


def shards(
    queries, attention_key_rows, attention_value_rows, output_gradient, parent_block, seg_start
):
    local_tokens = queries.shape[0]
    local_blocks = local_tokens // BLOCK_TOKENS
    head_groups = QUERY_HEADS // KEY_VALUE_HEADS
    kv_width = KEY_VALUE_HEADS * HEAD_SIZE
    score_scale = HEAD_SIZE ** (-0.5)
    device_id = lax.axis_index("ctx")
    first_here = device_id * local_blocks
    first_window = (device_id - (PARENT_SHARDS - 1)) * local_blocks
    parent_here = lax.dynamic_slice_in_dim(parent_block, first_here, local_blocks)
    start_here = lax.dynamic_slice_in_dim(seg_start, first_here, local_blocks)
    table_ids = jnp.arange(parent_block.shape[0])
    picked = parent_here[:, None] == table_ids[None, :]
    start_parent = jnp.sum(jnp.where(picked, seg_start[None, :], 0), axis=1)
    key_masks = block_masks(parent_here, start_here, start_parent)
    window_slot = jnp.clip(parent_here - first_window, 0, PARENT_SHARDS * local_blocks - 1)
    key_value_pair = jnp.stack([attention_key_rows, attention_value_rows])
    pieces = [
        from_behind(key_value_pair, "ctx", distance) for distance in range(PARENT_SHARDS - 1, 0, -1)
    ]
    window_span = jnp.concatenate(pieces + [key_value_pair], axis=1)
    window_block_rows = window_span.reshape(2, PARENT_SHARDS * local_blocks, BLOCK_TOKENS, kv_width)
    far_pair = jnp.take(window_block_rows, window_slot, axis=1)
    local_key_value = key_value_pair.reshape(2, local_blocks, BLOCK_TOKENS, kv_width)
    joined = jnp.concatenate([far_pair, local_key_value], axis=2)
    blocked_queries = queries.reshape(local_blocks, BLOCK_TOKENS, QUERY_HEADS * HEAD_SIZE)
    gradient_blocks = output_gradient.reshape(local_blocks, BLOCK_TOKENS, QUERY_HEADS * HEAD_SIZE)

    def one_block(inputs):
        query_rows, grad_rows, key_rows, value_rows, mask_rows = inputs
        query_head = query_rows.reshape(BLOCK_TOKENS, KEY_VALUE_HEADS, head_groups, HEAD_SIZE)
        grad_head = grad_rows.reshape(BLOCK_TOKENS, KEY_VALUE_HEADS, head_groups, HEAD_SIZE)
        key_head = key_rows.reshape(2 * BLOCK_TOKENS, KEY_VALUE_HEADS, HEAD_SIZE)
        value_head = value_rows.reshape(2 * BLOCK_TOKENS, KEY_VALUE_HEADS, HEAD_SIZE)
        scores = (
            jnp.einsum("ihgd,jhd->hgij", query_head, key_head, preferred_element_type=jnp.float32)
            * score_scale
        )
        masked = jnp.where(mask_rows[None, None], scores, NEG_FILL)
        row_max = jnp.max(masked, axis=-1, keepdims=True)
        weight = jnp.exp(masked - row_max)
        attn_prob = weight / jnp.sum(weight, axis=-1, keepdims=True)
        prob_low = attn_prob.astype(jnp.bfloat16)
        output = jnp.einsum(
            "hgij,jhd->ihgd", prob_low, value_head, preferred_element_type=jnp.float32
        ).astype(jnp.bfloat16)
        output = lax.optimization_barrier(output)
        row_delta = jnp.sum(grad_head.astype(jnp.float32) * output.astype(jnp.float32), axis=-1)
        grad_prob = jnp.einsum(
            "ihgd,jhd->hgij", grad_head, value_head, preferred_element_type=jnp.float32
        )
        grad_score = attn_prob * (grad_prob - jnp.transpose(row_delta, (1, 2, 0))[..., None])
        score_low = grad_score.astype(jnp.bfloat16)
        query_part = (
            jnp.einsum("hgij,jhd->ihgd", score_low, key_head, preferred_element_type=jnp.float32)
            * score_scale
        ).astype(jnp.bfloat16)
        key_part = (
            jnp.einsum("hgij,ihgd->jhd", score_low, query_head, preferred_element_type=jnp.float32)
            * score_scale
        )
        value_part = jnp.einsum(
            "hgij,ihgd->jhd", prob_low, grad_head, preferred_element_type=jnp.float32
        )
        return (
            query_part.reshape(BLOCK_TOKENS, QUERY_HEADS * HEAD_SIZE),
            key_part.reshape(2 * BLOCK_TOKENS, kv_width),
            value_part.reshape(2 * BLOCK_TOKENS, kv_width),
        )

    query_gradient, key_gradient, value_gradient = lax.map(
        one_block, (blocked_queries, gradient_blocks, joined[0], joined[1], key_masks)
    )
    far_flat = jnp.stack(
        [key_gradient[:, :BLOCK_TOKENS], value_gradient[:, :BLOCK_TOKENS]]
    ).reshape(2, local_blocks, BLOCK_TOKENS * kv_width)
    owners = (
        (window_slot[None, :] == jnp.arange(PARENT_SHARDS * local_blocks)[:, None])
        & (parent_here[None, :] >= 0)
    ).astype(jnp.float32)
    window_gradient = jnp.einsum("wb,xbc->xwc", owners, far_flat, precision=lax.Precision.HIGHEST)
    window_gradient = window_gradient.reshape(2, PARENT_SHARDS * local_tokens, kv_width)
    returned = window_gradient[:, (PARENT_SHARDS - 1) * local_tokens :]
    for distance in range(1, PARENT_SHARDS):
        start_row = (PARENT_SHARDS - 1 - distance) * local_tokens
        returned = returned + from_behind(
            window_gradient[:, start_row : start_row + local_tokens].astype(jnp.bfloat16),
            "ctx",
            -distance,
        ).astype(jnp.float32)
    own_grads = jnp.stack(
        [key_gradient[:, BLOCK_TOKENS:], value_gradient[:, BLOCK_TOKENS:]]
    ).reshape(2, local_tokens, kv_width)
    pair_grads = (own_grads + returned).astype(jnp.bfloat16)
    grad_queries = query_gradient.reshape(local_tokens, QUERY_HEADS * HEAD_SIZE)
    return (grad_queries, pair_grads[0], pair_grads[1])


def solution(mesh):
    placed = (P("ctx", None), P("ctx", None), P("ctx", None), P("ctx", None), P(), P())
    return jax.shard_map(
        shards,
        mesh=mesh,
        in_specs=placed,
        out_specs=(P("ctx", None), P("ctx", None), P("ctx", None)),
        check_vma=False,
    )
```

profile of v0, /device:TPU:126, one launch (start us, length us, event | category | flops | bytes accessed | tf_op | source)
XLA Modules:
  0.0 163.0 jit_solution(4046555876316558744)
XLA Ops:
  0.6 1.1 pad_maximum_fusion
  1.7 1.9 %collective-permute-start.2 = (bf16[2,512,256]{2,1,0:T(8,128)(2,1)S(1)}, bf16[2,512,256]{2,1,0:T(8,128)(2,1)S(1)}, u32[]{:S(2)}, u32[]{:S(2)}) collective-permute-start(bf16[2,512,256]{2,1,0:T(8,128)(2,1)S(1)} %pad_maximum_fusion), channel_id=1, source_target_pairs={{0,1},{1,2},{2,3},{3,4},{4,5},{5,6},{6,7},{7,8},{8,9},{9,10},{10,1... | collective-permute-start | bytes 1572872 | tf_op jit(solution)/shard_map/ppermute | solution.py:19
  3.6 5.0 %collective-permute-start.1 = (bf16[2,512,256]{2,1,0:T(8,128)(2,1)S(1)}, bf16[2,512,256]{2,1,0:T(8,128)(2,1)S(1)}, u32[]{:S(2)}, u32[]{:S(2)}) collective-permute-start(bf16[2,512,256]{2,1,0:T(8,128)(2,1)S(1)} %pad_maximum_fusion), channel_id=1, source_target_pairs={{0,2},{1,3},{2,4},{3,5},{4,6},{5,7},{6,8},{7,9},{8,10},{9,11},{10,... | collective-permute-start | bytes 1572872 | tf_op jit(solution)/shard_map/ppermute | solution.py:19
  8.6 4.3 %collective-permute-start = (bf16[2,512,256]{2,1,0:T(8,128)(2,1)S(1)}, bf16[2,512,256]{2,1,0:T(8,128)(2,1)}, u32[]{:S(2)}, u32[]{:S(2)}) collective-permute-start(bf16[2,512,256]{2,1,0:T(8,128)(2,1)S(1)} %pad_maximum_fusion), channel_id=1, source_target_pairs={{0,3},{1,4},{2,5},{3,6},{4,7},{5,8},{6,9},{7,10},{8,11},{9,12},{10... | collective-permute-start | bytes 1572872 | tf_op jit(solution)/shard_map/ppermute | solution.py:19
  13.8 0.9 select_reduce_fusion
  15.2 4.7 %collective-permute-done.2 = bf16[2,512,256]{2,1,0:T(8,128)(2,1)S(1)} collective-permute-done((bf16[2,512,256]{2,1,0:T(8,128)(2,1)S(1)}, bf16[2,512,256]{2,1,0:T(8,128)(2,1)S(1)}, u32[]{:S(2)}, u32[]{:S(2)}) %collective-permute-start.2) | collective-permute-done | bytes 524320 | tf_op jit(solution)/shard_map/ppermute | solution.py:19
  19.9 6.7 %collective-permute-done.1 = bf16[2,512,256]{2,1,0:T(8,128)(2,1)S(1)} collective-permute-done((bf16[2,512,256]{2,1,0:T(8,128)(2,1)S(1)}, bf16[2,512,256]{2,1,0:T(8,128)(2,1)S(1)}, u32[]{:S(2)}, u32[]{:S(2)}) %collective-permute-start.1) | collective-permute-done | bytes 524320 | tf_op jit(solution)/shard_map/ppermute | solution.py:19
  26.5 11.2 %collective-permute-done = bf16[2,512,256]{2,1,0:T(8,128)(2,1)} collective-permute-done((bf16[2,512,256]{2,1,0:T(8,128)(2,1)S(1)}, bf16[2,512,256]{2,1,0:T(8,128)(2,1)}, u32[]{:S(2)}, u32[]{:S(2)}) %collective-permute-start) | collective-permute-done | bytes 524320 | tf_op jit(solution)/shard_map/ppermute | solution.py:19
  37.8 1.5 maximum_maximum_fusion
  40.4 60.8 %while.14 = (s32[]{:T(128)}, bf16[4,128,2048]{2,1,0:T(8,128)(2,1)}, f32[4,256,256]{1,2,0:T(8,128)}, f32[4,256,256]{1,2,0:T(8,128)}, bf16[4,256,256]{2,1,0:T(8,12...) while((s32[]{:T(128)}, bf16[4,128,2048]{2,1,0:T(8,128)(2,1)}, ...), condition=%wide.region_5.6_spmd, body=%wide.region_1.0_spmd.sunk | while | flops 817688832 | bytes 55754916 | solution.py:107
  40.7 1.1 constant_dynamic-slice_fusion.10
  42.1 1.1 constant_dynamic-slice_fusion.11
  43.4 3.3 %fusion.80 = (f32[4,8,128]{2,1,0:T(8,128)S(1)}, f32[4,8,128,256]{2,3,1,0:T(8,128)}) fusion(pred[128,256]{0,1:T(8,128)(4,1)S(1)} %dynamic-slice_bitcast_fusion.2, bf16[256,4,64,1]{0,2,3,1:T(8,128)(2,1)S(1)} %bitcast.152, bf16[128,4,8,64]{0,3,2,1:T(8,128)(2,1)S(1)} %bitcast.147), kind=kOutput, calls=%fused_computation.72.clone.1 | convolution fusion | flops 138412288 | bytes 4898816 | tf_op jit(solution)/shard_map/while/body/eval_jaxpr/sub | solution.py:77
  46.8 2.7 %fusion.81 = bf16[4,8,128,256]{2,3,1,0:T(8,128)(2,1)S(1)} fusion(f32[4,8,128,256]{2,3,1,0:T(8,128)} %get-tuple-element.175, f32[4,8,128]{2,1,0:T(8,128)S(1)} %get-tuple-element.176), kind=kLoop, calls=%fused_computation.12.clone.1 | loop fusion | flops 2097152 | bytes 6307840 | tf_op jit(solution)/shard_map/while/body/eval_jaxpr/convert_element_type | solution.py:79
  51.7 0.9 fusion.83
  54.0 0.8 constant_dynamic-update-slice_fusion.5
  54.8 0.9 constant_dynamic-update-slice_fusion.6
  55.9 1.1 constant_dynamic-slice_fusion.10
  57.3 1.1 constant_dynamic-slice_fusion.11
  58.7 3.3 %fusion.80 = (f32[4,8,128]{2,1,0:T(8,128)S(1)}, f32[4,8,128,256]{2,3,1,0:T(8,128)}) fusion(pred[128,256]{0,1:T(8,128)(4,1)S(1)} %dynamic-slice_bitcast_fusion.2, bf16[256,4,64,1]{0,2,3,1:T(8,128)(2,1)S(1)} %bitcast.152, bf16[128,4,8,64]{0,3,2,1:T(8,128)(2,1)S(1)} %bitcast.147), kind=kOutput, calls=%fused_computation.72.clone.1 | convolution fusion | flops 138412288 | bytes 4898816 | tf_op jit(solution)/shard_map/while/body/eval_jaxpr/sub | solution.py:77
  62.0 2.7 %fusion.81 = bf16[4,8,128,256]{2,3,1,0:T(8,128)(2,1)S(1)} fusion(f32[4,8,128,256]{2,3,1,0:T(8,128)} %get-tuple-element.175, f32[4,8,128]{2,1,0:T(8,128)S(1)} %get-tuple-element.176), kind=kLoop, calls=%fused_computation.12.clone.1 | loop fusion | flops 2097152 | bytes 6307840 | tf_op jit(solution)/shard_map/while/body/eval_jaxpr/convert_element_type | solution.py:79
  66.9 0.9 fusion.83
  69.2 0.8 constant_dynamic-update-slice_fusion.5
  70.0 0.9 constant_dynamic-update-slice_fusion.6
  71.1 1.1 constant_dynamic-slice_fusion.10
  72.5 1.1 constant_dynamic-slice_fusion.11
  73.9 3.3 %fusion.80 = (f32[4,8,128]{2,1,0:T(8,128)S(1)}, f32[4,8,128,256]{2,3,1,0:T(8,128)}) fusion(pred[128,256]{0,1:T(8,128)(4,1)S(1)} %dynamic-slice_bitcast_fusion.2, bf16[256,4,64,1]{0,2,3,1:T(8,128)(2,1)S(1)} %bitcast.152, bf16[128,4,8,64]{0,3,2,1:T(8,128)(2,1)S(1)} %bitcast.147), kind=kOutput, calls=%fused_computation.72.clone.1 | convolution fusion | flops 138412288 | bytes 4898816 | tf_op jit(solution)/shard_map/while/body/eval_jaxpr/sub | solution.py:77
  77.2 2.7 %fusion.81 = bf16[4,8,128,256]{2,3,1,0:T(8,128)(2,1)S(1)} fusion(f32[4,8,128,256]{2,3,1,0:T(8,128)} %get-tuple-element.175, f32[4,8,128]{2,1,0:T(8,128)S(1)} %get-tuple-element.176), kind=kLoop, calls=%fused_computation.12.clone.1 | loop fusion | flops 2097152 | bytes 6307840 | tf_op jit(solution)/shard_map/while/body/eval_jaxpr/convert_element_type | solution.py:79
  82.1 0.9 fusion.83
  84.4 0.8 constant_dynamic-update-slice_fusion.5
  85.2 0.9 constant_dynamic-update-slice_fusion.6
  86.4 1.1 constant_dynamic-slice_fusion.10
  87.7 1.1 constant_dynamic-slice_fusion.11
  89.1 3.3 %fusion.80 = (f32[4,8,128]{2,1,0:T(8,128)S(1)}, f32[4,8,128,256]{2,3,1,0:T(8,128)}) fusion(pred[128,256]{0,1:T(8,128)(4,1)S(1)} %dynamic-slice_bitcast_fusion.2, bf16[256,4,64,1]{0,2,3,1:T(8,128)(2,1)S(1)} %bitcast.152, bf16[128,4,8,64]{0,3,2,1:T(8,128)(2,1)S(1)} %bitcast.147), kind=kOutput, calls=%fused_computation.72.clone.1 | convolution fusion | flops 138412288 | bytes 4898816 | tf_op jit(solution)/shard_map/while/body/eval_jaxpr/sub | solution.py:77
  92.4 2.7 %fusion.81 = bf16[4,8,128,256]{2,3,1,0:T(8,128)(2,1)S(1)} fusion(f32[4,8,128,256]{2,3,1,0:T(8,128)} %get-tuple-element.175, f32[4,8,128]{2,1,0:T(8,128)S(1)} %get-tuple-element.176), kind=kLoop, calls=%fused_computation.12.clone.1 | loop fusion | flops 2097152 | bytes 6307840 | tf_op jit(solution)/shard_map/while/body/eval_jaxpr/convert_element_type | solution.py:79
  97.3 0.9 fusion.83
  99.6 0.8 constant_dynamic-update-slice_fusion.5
  101.3 1.3 fusion.33
  103.0 1.3 fusion.32
  104.8 3.9 %convolution_bitcast_fusion.1 = f32[2,16,32768]{2,1,0:T(8,128)} fusion(f32[1,4,32768]{2,1,0:T(4,128)S(1)} %stack.43, f32[1,4,32768]{2,1,0:T(4,128)S(1)} %stack.42, s32[4]{0:T(128)S(1)} %get-tuple-element.96, pred[4]{0:T(512)(128)(4,1)S(1)} %get-tuple-element.114), kind=kOutput, calls=%fused_computation.31 | convolution fusion | flops 50593920 | bytes 5242900 | tf_op jit(solution)/shard_map/wb,xbc->xwc/dot_general | solution.py:117
  108.7 4.9 %reshape.229 = f32[2,2048,256]{2,1,0:T(8,128)} reshape(f32[2,16,32768]{2,1,0:T(8,128)} %convolution_bitcast_fusion.1) | data formatting | bytes 8388608 | tf_op jit(solution)/shard_map/reshape | solution.py:118
  113.6 2.4 %convert.5 = bf16[2,2048,256]{2,1,0:T(8,128)(2,1)S(1)} convert(f32[2,2048,256]{2,1,0:T(8,128)} %reshape.229) | non-fusion elementwise | flops 1048576 | bytes 6291456 | tf_op jit(solution)/shard_map/convert.2
  116.1 1.9 %collective-permute-start.3 = (bf16[2,512,256]{2,1,0:T(8,128)(2,1)S(1)}, bf16[2,512,256]{2,1,0:T(8,128)(2,1)}, u32[]{:S(2)}, u32[]{:S(2)}) collective-permute-start(bf16[2,512,256]{2,1,0:T(8,128)(2,1)S(1)} %get-tuple-element.101), channel_id=1, source_target_pairs={{1,0},{2,1},{3,2},{4,3},{5,4},{6,5},{7,6},{8,7},{9,8},{10,9},{11,1... | collective-permute-start | bytes 1572872 | tf_op jit(solution)/shard_map/ppermute | solution.py:19
  118.0 7.5 %collective-permute-start.5 = (bf16[2,512,256]{2,1,0:T(8,128)(2,1)S(1)}, bf16[2,512,256]{2,1,0:T(8,128)(2,1)}, u32[]{:S(2)}, u32[]{:S(2)}) collective-permute-start(bf16[2,512,256]{2,1,0:T(8,128)(2,1)S(1)} %get-tuple-element.102), channel_id=1, source_target_pairs={{3,0},{4,1},{5,2},{6,3},{7,4},{8,5},{9,6},{10,7},{11,8},{12,9},{13... | collective-permute-start | bytes 1572872 | tf_op jit(solution)/shard_map/ppermute | solution.py:19
  125.5 1.9 %collective-permute-start.4 = (bf16[2,512,256]{2,1,0:T(8,128)(2,1)S(1)}, bf16[2,512,256]{2,1,0:T(8,128)(2,1)}, u32[]{:S(2)}, u32[]{:S(2)}) collective-permute-start(bf16[2,512,256]{2,1,0:T(8,128)(2,1)S(1)} %get-tuple-element.103), channel_id=1, source_target_pairs={{2,0},{3,1},{4,2},{5,3},{6,4},{7,5},{8,6},{9,7},{10,8},{11,9},{12,... | collective-permute-start | bytes 1572872 | tf_op jit(solution)/shard_map/ppermute | solution.py:19
  127.8 14.3 %collective-permute-done.5 = bf16[2,512,256]{2,1,0:T(8,128)(2,1)} collective-permute-done((bf16[2,512,256]{2,1,0:T(8,128)(2,1)S(1)}, bf16[2,512,256]{2,1,0:T(8,128)(2,1)}, u32[]{:S(2)}, u32[]{:S(2)}) %collective-permute-start.5) | collective-permute-done | bytes 524320 | tf_op jit(solution)/shard_map/ppermute | solution.py:19
  142.2 18.1 %collective-permute-done.4 = bf16[2,512,256]{2,1,0:T(8,128)(2,1)} collective-permute-done((bf16[2,512,256]{2,1,0:T(8,128)(2,1)S(1)}, bf16[2,512,256]{2,1,0:T(8,128)(2,1)}, u32[]{:S(2)}, u32[]{:S(2)}) %collective-permute-start.4) | collective-permute-done | bytes 524320 | tf_op jit(solution)/shard_map/ppermute | solution.py:19
  160.2 1.9 %fusion.18 = bf16[2,512,256]{2,1,0:T(8,128)(2,1)S(1)} fusion(f32[2,2048,256]{2,1,0:T(8,128)} %reshape.229, f32[1,512,256]{2,1,0:T(8,128)S(1)} %bitcast.164, f32[1,512,256]{2,1,0:T(8,128)S(1)} %bitcast.165, bf16[2,512,256]{2,1,0:T(8,128)(2,1)} %collective-permute-done.5, bf16[2,512,256]{2,1,0:T(8,128)(2,1)} %collective-permute-done.4, ...), kind=kLoop, calls=%fused_computation.37 | loop fusion | flops 2359296 | bytes 4194304 | tf_op jit(solution)/shard_map/convert_element_type | solution.py:130
  (92 shorter events, 23.0 us)
Async XLA Ops:
  1.7 18.2 %collective-permute-start.2 = (bf16[2,512,256]{2,1,0:T(8,128)(2,1)S(1)}, bf16[2,512,256]{2,1,0:T(8,128)(2,1)S(1)}, u32[]{:S(2)}, u32[]{:S(2)}) collective-permute-start(bf16[2,512,256]{2,1,0:T(8,128)(2,1)S(1)} %pad_maximum_fusion), channel_id=1, source_target_pairs={{0,1},{1,2},{2,3},{3,4},{4,5},{5,6},{6,7},{7,8},{8,9},{9,10},{10,1... | collective-permute-start | bytes 1572872 | tf_op jit(solution)/shard_map/ppermute | solution.py:19
  3.6 22.9 %collective-permute-start.1 = (bf16[2,512,256]{2,1,0:T(8,128)(2,1)S(1)}, bf16[2,512,256]{2,1,0:T(8,128)(2,1)S(1)}, u32[]{:S(2)}, u32[]{:S(2)}) collective-permute-start(bf16[2,512,256]{2,1,0:T(8,128)(2,1)S(1)} %pad_maximum_fusion), channel_id=1, source_target_pairs={{0,2},{1,3},{2,4},{3,5},{4,6},{5,7},{6,8},{7,9},{8,10},{9,11},{10,... | collective-permute-start | bytes 1572872 | tf_op jit(solution)/shard_map/ppermute | solution.py:19
  8.6 29.2 %collective-permute-start = (bf16[2,512,256]{2,1,0:T(8,128)(2,1)S(1)}, bf16[2,512,256]{2,1,0:T(8,128)(2,1)}, u32[]{:S(2)}, u32[]{:S(2)}) collective-permute-start(bf16[2,512,256]{2,1,0:T(8,128)(2,1)S(1)} %pad_maximum_fusion), channel_id=1, source_target_pairs={{0,3},{1,4},{2,5},{3,6},{4,7},{5,8},{6,9},{7,10},{8,11},{9,12},{10... | collective-permute-start | bytes 1572872 | tf_op jit(solution)/shard_map/ppermute | solution.py:19
  39.2 1.0 copy-start.1
  39.3 1.0 copy-start.2
  49.5 2.2 %copy-start = (f32[4,8,128,256]{2,3,1,0:T(8,128)S(1)}, f32[4,8,128,256]{2,3,1,0:T(8,128)}, u32[]{:S(2)}) copy-start(f32[4,8,128,256]{2,3,1,0:T(8,128)} %get-tuple-element.175) | copy-start | bytes 12582916 | tf_op jit(solution)/shard_map/while
  64.7 2.2 %copy-start = (f32[4,8,128,256]{2,3,1,0:T(8,128)S(1)}, f32[4,8,128,256]{2,3,1,0:T(8,128)}, u32[]{:S(2)}) copy-start(f32[4,8,128,256]{2,3,1,0:T(8,128)} %get-tuple-element.175) | copy-start | bytes 12582916 | tf_op jit(solution)/shard_map/while
  79.9 2.2 %copy-start = (f32[4,8,128,256]{2,3,1,0:T(8,128)S(1)}, f32[4,8,128,256]{2,3,1,0:T(8,128)}, u32[]{:S(2)}) copy-start(f32[4,8,128,256]{2,3,1,0:T(8,128)} %get-tuple-element.175) | copy-start | bytes 12582916 | tf_op jit(solution)/shard_map/while
  95.1 2.2 %copy-start = (f32[4,8,128,256]{2,3,1,0:T(8,128)S(1)}, f32[4,8,128,256]{2,3,1,0:T(8,128)}, u32[]{:S(2)}) copy-start(f32[4,8,128,256]{2,3,1,0:T(8,128)} %get-tuple-element.175) | copy-start | bytes 12582916 | tf_op jit(solution)/shard_map/while
  116.1 11.8 %collective-permute-start.3 = (bf16[2,512,256]{2,1,0:T(8,128)(2,1)S(1)}, bf16[2,512,256]{2,1,0:T(8,128)(2,1)}, u32[]{:S(2)}, u32[]{:S(2)}) collective-permute-start(bf16[2,512,256]{2,1,0:T(8,128)(2,1)S(1)} %get-tuple-element.101), channel_id=1, source_target_pairs={{1,0},{2,1},{3,2},{4,3},{5,4},{6,5},{7,6},{8,7},{9,8},{10,9},{11,1... | collective-permute-start | bytes 1572872 | tf_op jit(solution)/shard_map/ppermute | solution.py:19
  118.0 24.2 %collective-permute-start.5 = (bf16[2,512,256]{2,1,0:T(8,128)(2,1)S(1)}, bf16[2,512,256]{2,1,0:T(8,128)(2,1)}, u32[]{:S(2)}, u32[]{:S(2)}) collective-permute-start(bf16[2,512,256]{2,1,0:T(8,128)(2,1)S(1)} %get-tuple-element.102), channel_id=1, source_target_pairs={{3,0},{4,1},{5,2},{6,3},{7,4},{8,5},{9,6},{10,7},{11,8},{12,9},{13... | collective-permute-start | bytes 1572872 | tf_op jit(solution)/shard_map/ppermute | solution.py:19
  125.5 34.7 %collective-permute-start.4 = (bf16[2,512,256]{2,1,0:T(8,128)(2,1)S(1)}, bf16[2,512,256]{2,1,0:T(8,128)(2,1)}, u32[]{:S(2)}, u32[]{:S(2)}) collective-permute-start(bf16[2,512,256]{2,1,0:T(8,128)(2,1)S(1)} %get-tuple-element.103), channel_id=1, source_target_pairs={{2,0},{3,1},{4,2},{5,3},{6,4},{7,5},{8,6},{9,7},{10,8},{11,9},{12,... | collective-permute-start | bytes 1572872 | tf_op jit(solution)/shard_map/ppermute | solution.py:19
where the time goes:
time: 164 us; the launch traced here: 163 us
  waiting for transfers between devices  55 us (34%)
  local copies, waits for them, and re-layouts  32.8 us (20%)
  matrix products  30.4 us (19%)
  starting transfers between devices  22.5 us (14%)
  other arithmetic  20.9 us (13%)
    ppermute x6, waiting for transfers between devices, from_behind(): lax.ppermute(value, axis, [(source, source + steps) for source in range(f...  55 us
    ppermute x6, starting transfers between devices, from_behind(): lax.ppermute(value, axis, [(source, source + steps) for source in range(f...  22.5 us
    sub x4, matrix products, one_block(): weight = jnp.exp(masked - row_max)  13.3 us
    dynamic_slice x32, local copies, waits for them, and re-layouts, shards(): lax.map(one_block, (blocked_queries, gradient_blocks, joined[0], joined[1...  11.7 us
    convert_element_type x4, other arithmetic, one_block(): prob_low = attn_prob.astype(jnp.bfloat16)  10.8 us
    dynamic_update_slice x12, local copies, waits for them, and re-layouts, shards(): lax.map(one_block, (blocked_queries, gradient_blocks, joined[0], joined[1...  7.56 us
    reshape x1, local copies, waits for them, and re-layouts, shards(): window_gradient.reshape(2, PARENT_SHARDS * local_tokens, kv_width)  4.87 us
    dot_general x1, matrix products, shards(): jnp.einsum('wb,xbc->xwc', owners, far_flat, precision=lax.Precision.HIGHEST)  3.91 us
  transfers between devices with their start and end apart: 6, of which 5 were waited for; matrix products, arithmetic and copies ran while one was open for 2% of the time, Pallas kernels for 0%

commit v1 on v0

v1 whole, which is shorter than its diff:
```python
import jax
import jax.numpy as jnp
from jax import lax
from jax.experimental import pallas as pl
from jax.experimental.pallas import tpu as pltpu
from jax.sharding import PartitionSpec as P

HEADS = 4
BLOCK = 128
BLOCKS = 4
ROWS = BLOCK * BLOCKS
F32, BF16 = jnp.float32, jnp.bfloat16
SCALE = 0.125
EXP2_SCALE = SCALE * 1.4426950408889634
NT = (((1,), (1,)), ((), ()))
NN = (((1,), (0,)), ((), ()))
TN = (((0,), (0,)), ((), ()))
MESH = pl.DeviceIdType.MESH


def dot(a, b, dims):
    return lax.dot_general(a, b, dims, preferred_element_type=F32)


def iota(shape, dim):
    return lax.broadcasted_iota(jnp.int32, shape, dim)


def swap_halves(x):
    return jnp.concatenate([x[:, 64:], x[:, :64]], 1)


def compute_block(h, b, own_kv, far_kv, q_ref, o_ref, dq_ref, bias_ref, own_ref, far_ref):
    rows = pl.ds(pl.multiple_of(b * BLOCK, BLOCK), BLOCK)
    kv = jnp.concatenate([own_kv, far_kv], 0)
    vk = swap_halves(kv)
    low = iota((256, 128), 1) < 64
    zero = jnp.zeros_like(kv)
    keys = jnp.concatenate([jnp.where(low, kv, zero), jnp.where(low, zero, vk)], 0)
    values = jnp.concatenate([jnp.where(low, vk, zero), jnp.where(low, zero, kv)], 0)
    bias = bias_ref[b]
    bias = jnp.concatenate([bias, bias], 1)
    causal = iota((BLOCK, 256), 0) <= lax.rem(iota((BLOCK, 256), 1), BLOCK)
    causal_low = causal.astype(F32).astype(BF16)
    queries, grads, scores = [], [], []
    for quad in range(2):
        c = h * 512 + quad * 256
        qs = jnp.concatenate([q_ref[rows, c : c + 128], q_ref[rows, c + 128 : c + 256]], 0)
        os = jnp.concatenate([o_ref[rows, c : c + 128], o_ref[rows, c + 128 : c + 256]], 0)
        queries.append(qs)
        grads.append(os)
        scores.append((dot(keys, qs, NT), dot(values, os, NT)))
    g_parts, p_parts = ([], []), ([], [])
    for quad in range(2):
        c = h * 512 + quad * 256
        s_all, d_all = scores[quad]
        dq_t = []
        for odd in range(2):
            r = odd * 256
            s = jnp.where(causal, s_all[r : r + 128], s_all[r + 128 : r + 256]) + bias
            w = jnp.exp2((s - jnp.max(s, 0, keepdims=True)) * EXP2_SCALE)
            inv = 1.0 / jnp.sum(w, 0, keepdims=True)
            d = jnp.where(causal, d_all[r : r + 128], d_all[r + 128 : r + 256])
            delta = jnp.sum(w * d, 0, keepdims=True) * inv
            p = w * inv
            g = (p * (d - delta)).astype(BF16)
            p = p.astype(BF16)
            p_own, g_own = p * causal_low, g * causal_low
            p = jnp.concatenate([p_own, p - p_own], 0)
            g = jnp.concatenate([g_own, g - g_own], 0)
            p_parts[odd].append(p)
            g_parts[odd].append(g)
            dq_t.append(dot(kv[:, :64], g, TN))
        dq = jnp.concatenate(dq_t, 0) * SCALE
        dq_ref[rows, c : c + 128] = dq[:, :128].T.astype(BF16)
        dq_ref[rows, c + 128 : c + 256] = dq[:, 128:].T.astype(BF16)
    qs, os = jnp.concatenate(queries, 0), jnp.concatenate(grads, 0)
    k_even = dot(jnp.concatenate(g_parts[0], 1), qs, NN) * SCALE
    k_odd = dot(jnp.concatenate(g_parts[1], 1), qs, NN) * SCALE
    v_even = dot(jnp.concatenate(p_parts[0], 1), os, NN)
    v_odd = dot(jnp.concatenate(p_parts[1], 1), os, NN)
    out = jnp.where(low, k_even, v_odd) + swap_halves(jnp.where(low, v_even, k_odd))
    own_ref[h, rows, :] = out[:BLOCK]
    far_ref[h, rows, :] = out[BLOCK:]


def kernel(
    q_hbm, o_hbm, k_ref, v_ref, parent_ref, start_ref, dq_hbm, dk_ref, dv_ref,
    q_ref, o_ref, dq_ref, win0, win1, win2, win3, own_ref, far_ref, bias_ref, out_buf, in_buf,
    load_sem, store_sem, fwd_send, fwd_recv, back_send, back_recv,
):
    me = lax.axis_index("ctx")
    count = lax.axis_size("ctx")
    core = lax.rem(me, 2)
    wins = (win0, win1, win2, win3)

    def at(step):
        return lax.rem(me + count + step, count)

    barrier = pltpu.get_barrier_semaphore()
    for step in (1, 2, 3, -1, -2, -3):
        pl.semaphore_signal(barrier, inc=1, device_id=(at(step),), device_id_type=MESH)
    loads = [
        pltpu.make_async_copy(q_hbm, q_ref, load_sem.at[0]),
        pltpu.make_async_copy(o_hbm, o_ref, load_sem.at[1]),
    ]
    for copy in loads:
        copy.start()
    OWN, NEAR, MID, FAR = (pl.ds(12, 4), pl.ds(8, 4), pl.ds(4, 4), pl.ds(0, 4))
    for h in range(HEADS):
        lanes = slice(64 * h, 64 * h + 64)
        for b in range(BLOCKS):
            rows = slice(b * BLOCK, (b + 1) * BLOCK)
            wins[h][12 + b] = jnp.concatenate([k_ref[rows, lanes], v_ref[rows, lanes]], 1)
    first = me * BLOCKS
    parents = [parent_ref[first + b] for b in range(BLOCKS)]
    slots = [
        jnp.where(p >= 0, jnp.clip(p - (first - 3 * BLOCKS), 0, 4 * BLOCKS - 1), -1)
        for p in parents
    ]
    for b in range(BLOCKS):
        s = start_ref[first + b]
        s2 = start_ref[jnp.maximum(parents[b], 0)]
        jj, ii = iota((BLOCK, BLOCK), 0), iota((BLOCK, BLOCK), 1)
        upto = jnp.where(s == 0, BLOCK, s)
        from_key = jnp.where(parents[b] >= 0, s2, BLOCK)
        own = jnp.where((jj >= s) == (ii >= s), 0.0, -1e30)
        far = jnp.where((ii < upto) & (jj >= from_key), 0.0, -1e30)
        bias_ref[b] = jnp.where(jj <= ii, own, far)
    pl.semaphore_wait(barrier, 6)

    def fwd(h, src, dst, send, recv, step):
        return pltpu.make_async_remote_copy(
            src_ref=wins[h].at[src], dst_ref=wins[h].at[dst],
            send_sem=fwd_send.at[h, send], recv_sem=fwd_recv.at[h, recv],
            device_id=(at(step),), device_id_type=MESH,
        )

    def send_own(h):
        @pl.when(core == 0)
        def _():
            fwd(h, OWN, FAR, 1, 2, 3).start()
        fwd(h, OWN, NEAR, 0, 0, 1).start()

    def relay(h):
        @pl.when(core == 0)
        def _():
            fwd(h, OWN, NEAR, 0, 0, 1).wait_recv()
            fwd(h, NEAR, FAR, 3, 2, 2).start()
            fwd(h, NEAR, MID, 2, 1, 1).start()

        @pl.when(core == 1)
        def _():
            fwd(h, OWN, FAR, 1, 2, 3).wait_recv()
            fwd(h, FAR, MID, 2, 1, -1).start()

    def ready(h):
        fwd(h, NEAR, MID, 2, 1, 1).wait_recv()

        @pl.when(core == 0)
        def _():
            fwd(h, NEAR, FAR, 3, 2, 2).wait_recv()

        @pl.when(core == 1)
        def _():
            fwd(h, OWN, NEAR, 0, 0, 1).wait_recv()

    def back(h, src, dst, step):
        return pltpu.make_async_remote_copy(
            src_ref=out_buf.at[h, src], dst_ref=in_buf.at[h, dst],
            send_sem=back_send.at[h, src], recv_sem=back_recv.at[h, dst],
            device_id=(at(step),), device_id_type=MESH,
        )

    def window_sum(h, distance, w):
        total = None
        for b in range(BLOCKS):
            if distance == 0 and w >= b:
                continue
            hit = jnp.where(slots[b] == (3 - distance) * BLOCKS + w, 1.0, 0.0)
            term = far_ref[h, b * BLOCK : (b + 1) * BLOCK, :] * hit
            total = term if total is None else total + term
        return total

    def block_rows(w):
        return slice(w * BLOCK, (w + 1) * BLOCK)

    def fill(h, src, distance, arrived):
        for w in range(BLOCKS):
            total = window_sum(h, distance, w)
            for dst in arrived:
                total = total + in_buf[h, dst, block_rows(w), :].astype(F32)
            out_buf[h, src, block_rows(w), :] = total.astype(BF16)

    def give(h):
        @pl.when(core == 0)
        def _():
            fill(h, 0, 3, ())
            back(h, 0, 1, -2).start()
            fill(h, 1, 2, ())
            back(h, 1, 0, 1).start()

        @pl.when(core == 1)
        def _():
            fill(h, 0, 2, ())
            back(h, 0, 0, -1).start()
            fill(h, 1, 1, ())
            back(h, 1, 2, -1).start()

    def merge(h):
        @pl.when(core == 0)
        def _():
            back(h, 0, 0, -1).wait_recv()
            back(h, 0, 1, -2).wait_recv()
            fill(h, 2, 1, (0, 1))
            back(h, 2, 2, -1).start()

        @pl.when(core == 1)
        def _():
            back(h, 1, 0, 1).wait_recv()
            fill(h, 2, 3, (0,))
            back(h, 2, 3, -3).start()

    def take(h):
        for w in range(BLOCKS - 1):
            own_ref[h, block_rows(w), :] += window_sum(h, 0, w)
        back(h, 1, 2, -1).wait_recv()

        @pl.when(core == 0)
        def _():
            back(h, 2, 3, -3).wait_recv()
            own_ref[h] += in_buf[h, 3].astype(F32)
        own_ref[h] += in_buf[h, 2].astype(F32)

    send_own(0)
    send_own(1)
    relay(0)
    send_own(2)
    for copy in loads:
        copy.wait()
    stores = []
    for h in range(HEADS):
        ready(h)

        @pl.loop(0, BLOCKS)
        def _(b, h=h):
            slot = jnp.maximum(parent_ref[first + b] - (first - 3 * BLOCKS), 0)
            own_kv = wins[h][12 + b]
            far_kv = wins[h][slot]
            compute_block(h, b, own_kv, far_kv, q_ref, o_ref, dq_ref, bias_ref, own_ref, far_ref)

            @pl.when(b == 0)
            def _():
                if h + 1 < HEADS:
                    relay(h + 1)
                if h + 3 < HEADS:
                    send_own(h + 3)

            @pl.when(b == 2)
            def _():
                if h > 0:
                    merge(h - 1)

        give(h)
        lanes = pl.ds(512 * h, 512)
        store = pltpu.make_async_copy(dq_ref.at[:, lanes], dq_hbm.at[:, lanes], store_sem.at[h])
        store.start()
        stores.append(store)
    for h in range(HEADS - 1):
        take(h)
    merge(HEADS - 1)
    take(HEADS - 1)
    for h in range(0, HEADS, 2):
        lanes = slice(64 * h, 64 * h + 128)
        a, b = own_ref[h], own_ref[h + 1]
        dk_ref[:, lanes] = jnp.concatenate([a[:, :64], b[:, :64]], 1).astype(BF16)
        dv_ref[:, lanes] = jnp.concatenate([a[:, 64:], b[:, 64:]], 1).astype(BF16)
    for copy in stores:
        copy.wait()
    for h in range(HEADS):
        fwd(h, OWN, NEAR, 0, 0, 1).wait_send()
        fwd(h, NEAR, MID, 2, 1, 1).wait_send()

        @pl.when(core == 0)
        def _():
            fwd(h, OWN, FAR, 1, 2, 3).wait_send()
            fwd(h, NEAR, FAR, 3, 2, 2).wait_send()
        for src in range(3):
            back(h, src, 0, 1).wait_send()


def shards(q, k, v, o, parent_block, seg_start):
    vmem = pl.BlockSpec(memory_space=pltpu.VMEM)
    smem = pl.BlockSpec(memory_space=pltpu.SMEM)
    hbm = pl.BlockSpec(memory_space=pl.ANY)
    width = q.shape[1]
    return pl.pallas_call(
        kernel,
        out_shape=(
            jax.ShapeDtypeStruct(q.shape, BF16),
            jax.ShapeDtypeStruct(k.shape, BF16),
            jax.ShapeDtypeStruct(v.shape, BF16),
        ),
        in_specs=[hbm, hbm, vmem, vmem, smem, smem],
        out_specs=(hbm, vmem, vmem),
        scratch_shapes=[
            pltpu.VMEM((ROWS, width), BF16),
            pltpu.VMEM((ROWS, width), BF16),
            pltpu.VMEM((ROWS, width), BF16),
        ]
        + [pltpu.VMEM((4 * BLOCKS, BLOCK, BLOCK), BF16)] * HEADS
        + [
            pltpu.VMEM((HEADS, ROWS, BLOCK), F32),
            pltpu.VMEM((HEADS, ROWS, BLOCK), F32),
            pltpu.VMEM((BLOCKS, BLOCK, BLOCK), F32),
            pltpu.VMEM((HEADS, 3, ROWS, BLOCK), BF16),
            pltpu.VMEM((HEADS, 4, ROWS, BLOCK), BF16),
            pltpu.SemaphoreType.DMA((2,)),
            pltpu.SemaphoreType.DMA((HEADS,)),
            pltpu.SemaphoreType.DMA((HEADS, 4)),
            pltpu.SemaphoreType.DMA((HEADS, 3)),
            pltpu.SemaphoreType.DMA((HEADS, 3)),
            pltpu.SemaphoreType.DMA((HEADS, 4)),
        ],
        compiler_params=pltpu.CompilerParams(
            collective_id=0, has_side_effects=True, vmem_limit_bytes=48 * 2**20
        ),
    )(q, o, k, v, parent_block, seg_start)


def solution(mesh):
    rows = P("ctx", None)
    return jax.shard_map(
        shards,
        mesh=mesh,
        in_specs=(rows, rows, rows, rows, P(), P()),
        out_specs=(rows, rows, rows),
        check_vma=False,
    )
```

time: 164 us -> 61.1 us (0.37)
  the two profiles are of different devices: /device:TPU:126 before, /device:TPU:1 now
where the time goes in v1:
time: 61.1 us; the launch traced here: 60.9 us
  Pallas kernels  52.6 us (86%)
  local copies, waits for them, and re-layouts  7.58 us (12%)
  between operations  0.65 us (1%)
    pallas_call x1, Pallas kernels, shards(): pl.pallas_call(kernel, out_shape=(jax.ShapeDtypeStruct(q.shape, BF16), ja...  52.6 us
    unnamed x13, local copies, waits for them, and re-layouts  7.58 us

profile of v1, /device:TPU:1, one launch (start us, length us, event | category | flops | bytes accessed | tf_op | source)
XLA Modules:
  0.0 60.9 jit_solution(12161754416395767262)
XLA Ops:
  0.6 0.0 copy-start
  0.6 1.6 %copy-done = bf16[512,2048]{1,0:T(8,128)(2,1)S(1)} copy-done((bf16[512,2048]{1,0:T(8,128)(2,1)S(1)}, bf16[512,2048]{1,0:T(8,128)(2,1)}, u32[]{:S(2)}) %copy-start) | copy-done | bytes 2097176
  2.2 0.0 copy-start.1
  2.2 0.9 %copy-done.1 = bf16[512,256]{1,0:T(8,128)(2,1)S(1)} copy-done((bf16[512,256]{1,0:T(8,128)(2,1)S(1)}, bf16[512,256]{1,0:T(8,128)(2,1)}, u32[]{:S(2)}) %copy-start.1) | copy-done | bytes 262168
  3.2 0.0 copy-start.2
  3.2 0.9 %copy-done.2 = bf16[512,256]{1,0:T(8,128)(2,1)S(1)} copy-done((bf16[512,256]{1,0:T(8,128)(2,1)S(1)}, bf16[512,256]{1,0:T(8,128)(2,1)}, u32[]{:S(2)}) %copy-start.2) | copy-done | bytes 262168
  4.1 0.0 copy-start.3
  4.1 0.7 %copy-done.3 = s32[1024]{0:T(1024)S(1)} copy-done((s32[1024]{0:T(1024)S(1)}, s32[1024]{0:T(1024)}, u32[]{:S(2)}) %copy-start.3) | copy-done | bytes 4120
  4.8 0.0 copy-start.4
  4.8 0.7 %copy-done.4 = s32[1024]{0:T(1024)S(1)} copy-done((s32[1024]{0:T(1024)S(1)}, s32[1024]{0:T(1024)}, u32[]{:S(2)}) %copy-start.4) | copy-done | bytes 4120
  5.5 52.6 %shard_map.85 = (bf16[512,2048]{1,0:T(8,128)(2,1)S(1)}, bf16[512,256]{1,0:T(8,128)(2,1)S(1)}, bf16[512,256]{1,0:T(8,128)(2,1)S(1)}) custom-call(bf16[512,2048]{1,0:T(8,128)(2,1)S(1)} %copy-done, bf16[512,2048]{1,0:T(8,128)(2,1)} %o_hbm.1, bf16[512,256]{1,0:T(8,128)(2,1)S(1)} %copy-done.1, bf16[512,256]{1,0:T(8,128)(2,1)S(1)} %copy-done.2, ...), custom_call_target="tpu_custom_call" | custom-call | tf_op jit(solution)/shard_map/pallas_call | solution.py:297
  58.1 1.3 %copy.12 = bf16[512,2048]{1,0:T(8,128)(2,1)} copy(bf16[512,2048]{1,0:T(8,128)(2,1)S(1)} %get-tuple-element.6) | data formatting | bytes 4194304
  59.5 0.7 %copy.13 = bf16[512,256]{1,0:T(8,128)(2,1)} copy(bf16[512,256]{1,0:T(8,128)(2,1)S(1)} %get-tuple-element.7) | data formatting | bytes 524288
  60.2 0.7 %copy.14 = bf16[512,256]{1,0:T(8,128)(2,1)} copy(bf16[512,256]{1,0:T(8,128)(2,1)S(1)} %get-tuple-element.8) | data formatting | bytes 524288
Async XLA Ops:
  0.6 1.6 %copy-start = (bf16[512,2048]{1,0:T(8,128)(2,1)S(1)}, bf16[512,2048]{1,0:T(8,128)(2,1)}, u32[]{:S(2)}) copy-start(bf16[512,2048]{1,0:T(8,128)(2,1)} %q_hbm.1) | copy-start | bytes 6291460
  2.2 0.9 %copy-start.1 = (bf16[512,256]{1,0:T(8,128)(2,1)S(1)}, bf16[512,256]{1,0:T(8,128)(2,1)}, u32[]{:S(2)}) copy-start(bf16[512,256]{1,0:T(8,128)(2,1)} %k_ref.1) | copy-start | bytes 786436
  3.2 0.9 %copy-start.2 = (bf16[512,256]{1,0:T(8,128)(2,1)S(1)}, bf16[512,256]{1,0:T(8,128)(2,1)}, u32[]{:S(2)}) copy-start(bf16[512,256]{1,0:T(8,128)(2,1)} %v_ref.1) | copy-start | bytes 786436
  4.1 0.7 %copy-start.3 = (s32[1024]{0:T(1024)S(1)}, s32[1024]{0:T(1024)}, u32[]{:S(2)}) copy-start(s32[1024]{0:T(1024)} %parent_ref.1) | copy-start | bytes 12292
  4.8 0.7 %copy-start.4 = (s32[1024]{0:T(1024)S(1)}, s32[1024]{0:T(1024)}, u32[]{:S(2)}) copy-start(s32[1024]{0:T(1024)} %start_ref.1) | copy-start | bytes 12292

commit v2 on v1

v2 whole, which is shorter than its diff:
```python
import jax
import jax.numpy as jnp
from jax import lax
from jax.experimental import pallas as pl
from jax.experimental.pallas import tpu as pltpu
from jax.sharding import PartitionSpec as P

HEADS = 4
BLOCK = 128
BLOCKS = 4
ROWS = BLOCK * BLOCKS
F32, BF16 = jnp.float32, jnp.bfloat16
SCALE = 0.125
EXP2_SCALE = SCALE * 1.4426950408889634
NT = (((1,), (1,)), ((), ()))
NN = (((1,), (0,)), ((), ()))
TN = (((0,), (0,)), ((), ()))
MESH = pl.DeviceIdType.MESH
OWN, NEAR, MID, FAR = 12, 8, 4, 0
FWD_PARTS = (4, 1, 1, 1)
BACK_PARTS = (1, 1, 1, 4)


def dot(a, b, dims):
    return lax.dot_general(a, b, dims, preferred_element_type=F32)


def iota(shape, dim):
    return lax.broadcasted_iota(jnp.int32, shape, dim)


def swap_halves(x):
    return jnp.concatenate([x[:, 64:], x[:, :64]], 1)


def compute_block(h, b, own_kv, far_kv, q_ref, o_ref, dq_ref, bias_ref, own_ref, far_ref):
    rows = pl.ds(pl.multiple_of(b * BLOCK, BLOCK), BLOCK)
    kv = jnp.concatenate([own_kv, far_kv], 0)
    vk = swap_halves(kv)
    low = iota((256, 128), 1) < 64
    zero = jnp.zeros_like(kv)
    keys = jnp.concatenate([jnp.where(low, kv, zero), jnp.where(low, zero, vk)], 0)
    values = jnp.concatenate([jnp.where(low, vk, zero), jnp.where(low, zero, kv)], 0)
    bias = bias_ref[b]
    bias = jnp.concatenate([bias, bias], 1)
    causal = iota((BLOCK, 256), 0) <= lax.rem(iota((BLOCK, 256), 1), BLOCK)
    causal_low = causal.astype(F32).astype(BF16)
    queries, grads, scores = [], [], []
    for quad in range(2):
        c = h * 512 + quad * 256
        qs = jnp.concatenate([q_ref[rows, c : c + 128], q_ref[rows, c + 128 : c + 256]], 0)
        os = jnp.concatenate([o_ref[rows, c : c + 128], o_ref[rows, c + 128 : c + 256]], 0)
        queries.append(qs)
        grads.append(os)
        scores.append((dot(keys, qs, NT), dot(values, os, NT)))
    g_parts, p_parts = ([], []), ([], [])
    for quad in range(2):
        c = h * 512 + quad * 256
        s_all, d_all = scores[quad]
        dq_t = []
        for odd in range(2):
            r = odd * 256
            s = jnp.where(causal, s_all[r : r + 128], s_all[r + 128 : r + 256]) + bias
            w = jnp.exp2((s - jnp.max(s, 0, keepdims=True)) * EXP2_SCALE)
            inv = 1.0 / jnp.sum(w, 0, keepdims=True)
            d = jnp.where(causal, d_all[r : r + 128], d_all[r + 128 : r + 256])
            delta = jnp.sum(w * d, 0, keepdims=True) * inv
            p = w * inv
            g = (p * (d - delta)).astype(BF16)
            p = p.astype(BF16)
            p_own, g_own = p * causal_low, g * causal_low
            p = jnp.concatenate([p_own, p - p_own], 0)
            g = jnp.concatenate([g_own, g - g_own], 0)
            p_parts[odd].append(p)
            g_parts[odd].append(g)
            dq_t.append(dot(kv[:, :64], g, TN))
        dq = jnp.concatenate(dq_t, 0) * SCALE
        dq_ref[rows, c : c + 128] = dq[:, :128].T.astype(BF16)
        dq_ref[rows, c + 128 : c + 256] = dq[:, 128:].T.astype(BF16)
    qs, os = jnp.concatenate(queries, 0), jnp.concatenate(grads, 0)
    k_even = dot(jnp.concatenate(g_parts[0], 1), qs, NN) * SCALE
    k_odd = dot(jnp.concatenate(g_parts[1], 1), qs, NN) * SCALE
    v_even = dot(jnp.concatenate(p_parts[0], 1), os, NN)
    v_odd = dot(jnp.concatenate(p_parts[1], 1), os, NN)
    out = jnp.where(low, k_even, v_odd) + swap_halves(jnp.where(low, v_even, k_odd))
    own_ref[h, rows, :] = out[:BLOCK]
    far_ref[h, rows, :] = out[BLOCK:]


def kernel(
    q_hbm, o_hbm, k_hbm, v_hbm, parent_hbm, start_hbm, dq_ref, dk_ref, dv_ref,
    k_ref, v_ref, parent_ref, start_ref, q_ref, o_ref, win0, win1, win2, win3, own_ref, far_ref, bias_ref, out_buf, in_buf,
    load_sem, fwd_send, fwd_recv, back_send, back_recv,
):
    me = lax.axis_index("ctx")
    count = lax.axis_size("ctx")
    core = lax.rem(me, 2)
    wins = (win0, win1, win2, win3)

    def at(step):
        return lax.rem(me + count + step, count)

    barrier = pltpu.get_barrier_semaphore()
    for step in (1, 2, 3, -1, -2, -3):
        pl.semaphore_signal(barrier, inc=1, device_id=(at(step),), device_id_type=MESH)
    loads = [
        pltpu.make_async_copy(src, dst, load_sem.at[n])
        for n, (src, dst) in enumerate(
            (
                (k_hbm, k_ref), (v_hbm, v_ref), (parent_hbm, parent_ref),
                (start_hbm, start_ref), (q_hbm, q_ref), (o_hbm, o_ref),
            )
        )
    ]
    for copy in loads:
        copy.start()
    for copy in loads[:2]:
        copy.wait()

    def pack(h):
        lanes = slice(64 * h, 64 * h + 64)
        for b in range(BLOCKS):
            rows = slice(b * BLOCK, (b + 1) * BLOCK)
            wins[h][12 + b] = jnp.concatenate([k_ref[rows, lanes], v_ref[rows, lanes]], 1)
    pack(0)
    pl.semaphore_wait(barrier, 6)

    def fwd(h, part, src, dst, send, recv, step):
        size = BLOCKS // FWD_PARTS[h]
        return pltpu.make_async_remote_copy(
            src_ref=wins[h].at[pl.ds(src + part * size, size)],
            dst_ref=wins[h].at[pl.ds(dst + part * size, size)],
            send_sem=fwd_send.at[h, send, part], recv_sem=fwd_recv.at[h, recv, part],
            device_id=(at(step),), device_id_type=MESH,
        )

    def own_far(h, part):
        return fwd(h, part, OWN, FAR, 1, 2, 3)

    def own_near(h, part):
        return fwd(h, part, OWN, NEAR, 0, 0, 1)

    def near_far(h, part):
        return fwd(h, part, NEAR, FAR, 3, 2, 2)

    def near_mid(h, part):
        return fwd(h, part, NEAR, MID, 2, 1, 1)

    def far_mid(h, part):
        return fwd(h, part, FAR, MID, 2, 1, -1)

    def send_own(h, far=True, near=True):
        if far:
            @pl.when(core == 0)
            def _():
                for part in range(FWD_PARTS[h]):
                    own_far(h, part).start()
        if near:
            for part in range(FWD_PARTS[h]):
                own_near(h, part).start()

    def relay(h):
        @pl.when(core == 0)
        def _():
            for part in range(FWD_PARTS[h]):
                own_near(h, part).wait_recv()
                near_far(h, part).start()
                near_mid(h, part).start()

        @pl.when(core == 1)
        def _():
            for part in range(FWD_PARTS[h]):
                own_far(h, part).wait_recv()
                far_mid(h, part).start()

    def ready(h):
        for part in range(FWD_PARTS[h]):
            near_mid(h, part).wait_recv()

            @pl.when(core == 0)
            def _():
                near_far(h, part).wait_recv()

            @pl.when(core == 1)
            def _():
                own_near(h, part).wait_recv()

    def back(h, part, src, dst, step):
        size = ROWS // BACK_PARTS[h]
        rows = pl.ds(part * size, size)
        return pltpu.make_async_remote_copy(
            src_ref=out_buf.at[h, src, rows], dst_ref=in_buf.at[h, dst, rows],
            send_sem=back_send.at[h, src, part], recv_sem=back_recv.at[h, dst, part],
            device_id=(at(step),), device_id_type=MESH,
        )

    def window_sum(h, distance, w):
        total = None
        for b in range(BLOCKS):
            if distance == 0 and w >= b:
                continue
            hit = jnp.where(slots[b] == (3 - distance) * BLOCKS + w, 1.0, 0.0)
            term = far_ref[h, b * BLOCK : (b + 1) * BLOCK, :] * hit
            total = term if total is None else total + term
        return total

    def block_rows(w):
        return slice(w * BLOCK, (w + 1) * BLOCK)

    def send(h, src, dst, step, distance, arrived):
        size = BLOCKS // BACK_PARTS[h]
        for part in range(BACK_PARTS[h]):
            for other in arrived:
                back(h, part, 0, other, 1).wait_recv()
            for w in range(part * size, (part + 1) * size):
                total = window_sum(h, distance, w)
                for other in arrived:
                    total = total + in_buf[h, other, block_rows(w), :].astype(F32)
                out_buf[h, src, block_rows(w), :] = total.astype(BF16)
            back(h, part, src, dst, step).start()

    def give(h):
        @pl.when(core == 0)
        def _():
            send(h, 0, 1, -2, 3, ())
            send(h, 1, 0, 1, 2, ())

        @pl.when(core == 1)
        def _():
            send(h, 0, 0, -1, 2, ())
            send(h, 1, 2, -1, 1, ())

    def merge_even(h):
        @pl.when(core == 0)
        def _():
            send(h, 2, 2, -1, 1, (0, 1))

    def merge_odd(h):
        @pl.when(core == 1)
        def _():
            send(h, 2, 3, -3, 3, (0,))

    def take(h):
        for w in range(BLOCKS - 1):
            own_ref[h, block_rows(w), :] += window_sum(h, 0, w)

        @pl.when(core == 0)
        def _():
            for part in range(BACK_PARTS[h]):
                back(h, part, 2, 3, -3).wait_recv()
            own_ref[h] += in_buf[h, 3].astype(F32)
        for part in range(BACK_PARTS[h]):
            back(h, part, 1, 2, -1).wait_recv()
        own_ref[h] += in_buf[h, 2].astype(F32)

    send_own(0)
    pack(1)
    send_own(1)
    pack(2)
    pack(3)
    for copy in loads[2:]:
        copy.wait()
    first = me * BLOCKS
    parents = [parent_ref[first + b] for b in range(BLOCKS)]
    slots = [
        jnp.where(p >= 0, jnp.clip(p - (first - 3 * BLOCKS), 0, 4 * BLOCKS - 1), -1)
        for p in parents
    ]
    for b in range(BLOCKS):
        s = start_ref[first + b]
        s2 = start_ref[jnp.maximum(parents[b], 0)]
        jj, ii = iota((BLOCK, BLOCK), 0), iota((BLOCK, BLOCK), 1)
        upto = jnp.where(s == 0, BLOCK, s)
        from_key = jnp.where(parents[b] >= 0, s2, BLOCK)
        own = jnp.where((jj >= s) == (ii >= s), 0.0, -1e30)
        far = jnp.where((ii < upto) & (jj >= from_key), 0.0, -1e30)
        bias_ref[b] = jnp.where(jj <= ii, own, far)
    relay(0)
    send_own(2, near=False)
    relay(1)
    send_own(2, far=False)
    send_own(3)
    for h in range(HEADS):
        ready(h)
        if h == 2:
            merge_even(0)

        @pl.loop(0, BLOCKS // 2)
        def _(pair, h=h):
            for b in (2 * pair, 2 * pair + 1):
                slot = jnp.maximum(parent_ref[first + b] - (first - 3 * BLOCKS), 0)
                compute_block(
                    h, b, wins[h][12 + b], wins[h][slot], q_ref, o_ref, dq_ref, bias_ref, own_ref, far_ref
                )

            @pl.when(pair == 0)
            def _():
                if h > 0:
                    merge_odd(h - 1)

        if h < 2:
            relay(h + 2)
        give(h)
        if h == 2:
            merge_even(1)
    merge_odd(3)
    merge_even(2)
    take(0)
    take(1)
    merge_even(3)
    take(2)
    take(3)
    for h in range(0, HEADS, 2):
        lanes = slice(64 * h, 64 * h + 128)
        a, b = own_ref[h], own_ref[h + 1]
        dk_ref[:, lanes] = jnp.concatenate([a[:, :64], b[:, :64]], 1).astype(BF16)
        dv_ref[:, lanes] = jnp.concatenate([a[:, 64:], b[:, 64:]], 1).astype(BF16)
    for h in range(HEADS):
        for part in range(FWD_PARTS[h]):
            own_near(h, part).wait_send()
            near_mid(h, part).wait_send()

            @pl.when(core == 0)
            def _():
                own_far(h, part).wait_send()
                near_far(h, part).wait_send()
        for part in range(BACK_PARTS[h]):
            for src in range(3):
                back(h, part, src, 0, 1).wait_send()


def shards(q, k, v, o, parent_block, seg_start):
    hbm = pl.BlockSpec(memory_space=pltpu.HBM)
    vmem = pl.BlockSpec(memory_space=pltpu.VMEM)
    width = q.shape[1]
    return pl.pallas_call(
        kernel,
        out_shape=(
            jax.ShapeDtypeStruct(q.shape, BF16),
            jax.ShapeDtypeStruct(k.shape, BF16),
            jax.ShapeDtypeStruct(v.shape, BF16),
        ),
        in_specs=[hbm] * 6,
        out_specs=(vmem,) * 3,
        scratch_shapes=[
            pltpu.VMEM(k.shape, BF16),
            pltpu.VMEM(v.shape, BF16),
            pltpu.SMEM(parent_block.shape, jnp.int32),
            pltpu.SMEM(seg_start.shape, jnp.int32),
            pltpu.VMEM((ROWS, width), BF16),
            pltpu.VMEM((ROWS, width), BF16),
        ]
        + [pltpu.VMEM((4 * BLOCKS, BLOCK, BLOCK), BF16)] * HEADS
        + [
            pltpu.VMEM((HEADS, ROWS, BLOCK), F32),
            pltpu.VMEM((HEADS, ROWS, BLOCK), F32),
            pltpu.VMEM((BLOCKS, BLOCK, BLOCK), F32),
            pltpu.VMEM((HEADS, 3, ROWS, BLOCK), BF16),
            pltpu.VMEM((HEADS, 4, ROWS, BLOCK), BF16),
            pltpu.SemaphoreType.DMA((6,)),
            pltpu.SemaphoreType.DMA((HEADS, 4, 4)),
            pltpu.SemaphoreType.DMA((HEADS, 3, 4)),
            pltpu.SemaphoreType.DMA((HEADS, 3, 4)),
            pltpu.SemaphoreType.DMA((HEADS, 4, 4)),
        ],
        compiler_params=pltpu.CompilerParams(
            collective_id=0, has_side_effects=True, vmem_limit_bytes=48 * 2**20
        ),
    )(*(pltpu.with_memory_space_constraint(x, pltpu.HBM) for x in (q, o, k, v, parent_block, seg_start)))


def solution(mesh):
    rows = P("ctx", None)
    return jax.shard_map(
        shards,
        mesh=mesh,
        in_specs=(rows, rows, rows, rows, P(), P()),
        out_specs=(rows, rows, rows),
        check_vma=False,
    )
```

time: 61.1 us -> 51.9 us (0.85)
  local copies, waits for them, and re-layouts: 7.58 us -> 2.73 us
  Pallas kernels: 52.6 us -> 48.4 us
    unnamed x13 -> x3, local copies, waits for them, and re-layouts: 7.58 us -> 2.73 us
    pallas_call x1, Pallas kernels: 52.6 us -> 48.4 us  [shards(): pl.pallas_call(kernel, out_shape=(jax.ShapeDtypeStruct(q.shape, BF16), ja...]
where the time goes in v2:
time: 51.9 us; the launch traced here: 51.8 us
  Pallas kernels  48.4 us (93%)
  local copies, waits for them, and re-layouts  2.73 us (5%)
  between operations  0.64 us (1%)
    pallas_call x1, Pallas kernels, shards(): pl.pallas_call(kernel, out_shape=(jax.ShapeDtypeStruct(q.shape, BF16), ja...  48.4 us
    unnamed x3, local copies, waits for them, and re-layouts  2.73 us

profile of v2, /device:TPU:1, one launch (start us, length us, event | category | flops | bytes accessed | tf_op | source)
XLA Modules:
  0.0 51.8 jit_solution(5747349308579603699)
XLA Ops:
  0.6 48.4 %shard_map.85 = (bf16[512,2048]{1,0:T(8,128)(2,1)S(1)}, bf16[512,256]{1,0:T(8,128)(2,1)S(1)}, bf16[512,256]{1,0:T(8,128)(2,1)S(1)}) custom-call(bf16[512,2048]{1,0:T(8,128)(2,1)} %q_hbm.1, bf16[512,2048]{1,0:T(8,128)(2,1)} %o_hbm.1, bf16[512,256]{1,0:T(8,128)(2,1)} %k_hbm.1, bf16[512,256]{1,0:T(8,128)(2,1)} %v_hbm.1, s32[1024]{0:T(1024)} %parent_hbm.1, ...), custom_call_target="tpu_custom_call" | custom-call | tf_op jit(solution)/shard_map/pallas_call | solution.py:336
  49.1 1.3 %copy.12 = bf16[512,2048]{1,0:T(8,128)(2,1)} copy(bf16[512,2048]{1,0:T(8,128)(2,1)S(1)} %get-tuple-element.6) | data formatting | bytes 4194304
  50.4 0.7 %copy.13 = bf16[512,256]{1,0:T(8,128)(2,1)} copy(bf16[512,256]{1,0:T(8,128)(2,1)S(1)} %get-tuple-element.7) | data formatting | bytes 524288
  51.1 0.7 %copy.14 = bf16[512,256]{1,0:T(8,128)(2,1)} copy(bf16[512,256]{1,0:T(8,128)(2,1)S(1)} %get-tuple-element.8) | data formatting | bytes 524288

commit v3 on v2

--- a/solution.py
+++ b/solution.py
@@ -34,7 +34,7 @@
 
 
 def compute_block(h, b, own_kv, far_kv, q_ref, o_ref, dq_ref, bias_ref, own_ref, far_ref):
-    rows = pl.ds(pl.multiple_of(b * BLOCK, BLOCK), BLOCK)
+    rows = slice(b * BLOCK, (b + 1) * BLOCK)
     kv = jnp.concatenate([own_kv, far_kv], 0)
     vk = swap_halves(kv)
     low = iota((256, 128), 1) < 64
@@ -97,12 +97,18 @@
     core = lax.rem(me, 2)
     wins = (win0, win1, win2, win3)
 
+    chip, last = me // 2, count // 2 - 1
+    even, odd = core == 0, core == 1
+    prev, prev2, later = chip > 0, chip > 1, chip < last
+
     def at(step):
         return lax.rem(me + count + step, count)
 
     barrier = pltpu.get_barrier_semaphore()
     for step in (1, 2, 3, -1, -2, -3):
-        pl.semaphore_signal(barrier, inc=1, device_id=(at(step),), device_id_type=MESH)
+        @pl.when(me + step < count if step > 0 else me + step >= 0)
+        def _():
+            pl.semaphore_signal(barrier, inc=1, device_id=(at(step),), device_id_type=MESH)
     loads = [
         pltpu.make_async_copy(src, dst, load_sem.at[n])
         for n, (src, dst) in enumerate(
@@ -123,7 +129,7 @@
             rows = slice(b * BLOCK, (b + 1) * BLOCK)
             wins[h][12 + b] = jnp.concatenate([k_ref[rows, lanes], v_ref[rows, lanes]], 1)
     pack(0)
-    pl.semaphore_wait(barrier, 6)
+    pl.semaphore_wait(barrier, jnp.minimum(me, 3) + jnp.minimum(count - 1 - me, 3))
 
     def fwd(h, part, src, dst, send, recv, step):
         size = BLOCKS // FWD_PARTS[h]
@@ -151,23 +157,28 @@
 
     def send_own(h, far=True, near=True):
         if far:
-            @pl.when(core == 0)
+            @pl.when(even & later)
             def _():
                 for part in range(FWD_PARTS[h]):
                     own_far(h, part).start()
         if near:
-            for part in range(FWD_PARTS[h]):
-                own_near(h, part).start()
+            @pl.when(even | later)
+            def _():
+                for part in range(FWD_PARTS[h]):
+                    own_near(h, part).start()
 
     def relay(h):
-        @pl.when(core == 0)
+        @pl.when(even & prev)
         def _():
             for part in range(FWD_PARTS[h]):
                 own_near(h, part).wait_recv()
-                near_far(h, part).start()
+
+                @pl.when(later)
+                def _():
+                    near_far(h, part).start()
                 near_mid(h, part).start()
 
-        @pl.when(core == 1)
+        @pl.when(odd & prev)
         def _():
             for part in range(FWD_PARTS[h]):
                 own_far(h, part).wait_recv()
@@ -175,15 +186,17 @@
 
     def ready(h):
         for part in range(FWD_PARTS[h]):
-            near_mid(h, part).wait_recv()
-
-            @pl.when(core == 0)
+            @pl.when(odd)
+            def _():
+                own_near(h, part).wait_recv()
+
+            @pl.when(prev)
+            def _():
+                near_mid(h, part).wait_recv()
+
+            @pl.when(even & prev2)
             def _():
                 near_far(h, part).wait_recv()
-
-            @pl.when(core == 1)
-            def _():
-                own_near(h, part).wait_recv()
 
     def back(h, part, src, dst, step):
         size = ROWS // BACK_PARTS[h]
@@ -220,23 +233,33 @@
             back(h, part, src, dst, step).start()
 
     def give(h):
-        @pl.when(core == 0)
+        @pl.when(even & prev2)
         def _():
             send(h, 0, 1, -2, 3, ())
+
+        @pl.when(even & prev)
+        def _():
             send(h, 1, 0, 1, 2, ())
 
-        @pl.when(core == 1)
+        @pl.when(odd & prev)
         def _():
             send(h, 0, 0, -1, 2, ())
+
+        @pl.when(odd)
+        def _():
             send(h, 1, 2, -1, 1, ())
 
     def merge_even(h):
-        @pl.when(core == 0)
+        @pl.when(even & prev & later)
         def _():
             send(h, 2, 2, -1, 1, (0, 1))
 
+        @pl.when(even & prev & (chip == last))
+        def _():
+            send(h, 2, 2, -1, 1, (0,))
+
     def merge_odd(h):
-        @pl.when(core == 1)
+        @pl.when(odd & prev)
         def _():
             send(h, 2, 3, -3, 3, (0,))
 
@@ -244,14 +267,17 @@
         for w in range(BLOCKS - 1):
             own_ref[h, block_rows(w), :] += window_sum(h, 0, w)
 
-        @pl.when(core == 0)
+        @pl.when(even & later)
         def _():
             for part in range(BACK_PARTS[h]):
                 back(h, part, 2, 3, -3).wait_recv()
             own_ref[h] += in_buf[h, 3].astype(F32)
-        for part in range(BACK_PARTS[h]):
-            back(h, part, 1, 2, -1).wait_recv()
-        own_ref[h] += in_buf[h, 2].astype(F32)
+
+        @pl.when(even | later)
+        def _():
+            for part in range(BACK_PARTS[h]):
+                back(h, part, 1, 2, -1).wait_recv()
+            own_ref[h] += in_buf[h, 2].astype(F32)
 
     send_own(0)
     pack(1)
@@ -261,6 +287,7 @@
     for copy in loads[2:]:
         copy.wait()
     first = me * BLOCKS
+    oldest = jnp.maximum(3 * BLOCKS - first, 0)
     parents = [parent_ref[first + b] for b in range(BLOCKS)]
     slots = [
         jnp.where(p >= 0, jnp.clip(p - (first - 3 * BLOCKS), 0, 4 * BLOCKS - 1), -1)
@@ -284,20 +311,15 @@
         ready(h)
         if h == 2:
             merge_even(0)
-
-        @pl.loop(0, BLOCKS // 2)
-        def _(pair, h=h):
-            for b in (2 * pair, 2 * pair + 1):
-                slot = jnp.maximum(parent_ref[first + b] - (first - 3 * BLOCKS), 0)
-                compute_block(
-                    h, b, wins[h][12 + b], wins[h][slot], q_ref, o_ref, dq_ref, bias_ref, own_ref, far_ref
-                )
-
-            @pl.when(pair == 0)
-            def _():
-                if h > 0:
-                    merge_odd(h - 1)
-
+        if h == 3:
+            merge_odd(2)
+        for b in range(BLOCKS):
+            slot = jnp.maximum(parent_ref[first + b] - (first - 3 * BLOCKS), oldest)
+            compute_block(
+                h, b, wins[h][12 + b], wins[h][slot], q_ref, o_ref, dq_ref, bias_ref, own_ref, far_ref
+            )
+        if h in (1, 2):
+            merge_odd(h - 1)
         if h < 2:
             relay(h + 2)
         give(h)
@@ -317,16 +339,33 @@
         dv_ref[:, lanes] = jnp.concatenate([a[:, 64:], b[:, 64:]], 1).astype(BF16)
     for h in range(HEADS):
         for part in range(FWD_PARTS[h]):
-            own_near(h, part).wait_send()
-            near_mid(h, part).wait_send()
-
-            @pl.when(core == 0)
+            @pl.when(even | later)
+            def _():
+                own_near(h, part).wait_send()
+
+            @pl.when(even & later)
             def _():
                 own_far(h, part).wait_send()
+
+            @pl.when(prev)
+            def _():
+                near_mid(h, part).wait_send()
+
+            @pl.when(even & prev & later)
+            def _():
                 near_far(h, part).wait_send()
         for part in range(BACK_PARTS[h]):
-            for src in range(3):
-                back(h, part, src, 0, 1).wait_send()
+            @pl.when(odd | prev)
+            def _():
+                back(h, part, 1, 0, 1).wait_send()
+
+            @pl.when((odd & prev) | prev2)
+            def _():
+                back(h, part, 0, 0, 1).wait_send()
+
+            @pl.when(prev)
+            def _():
+                back(h, part, 2, 0, 1).wait_send()
 
 
 def shards(q, k, v, o, parent_block, seg_start):

time: 51.9 us -> 48.5 us (0.934)
  the two profiles are of different devices: /device:TPU:1 before, /device:TPU:25 now
where the time goes in v3:
time: 48.5 us
  Pallas kernels  45.1 us (93%)
  local copies, waits for them, and re-layouts  2.73 us (6%)
  between operations  0.64 us (1%)
    pallas_call x1, Pallas kernels, shards(): pl.pallas_call(kernel, out_shape=(jax.ShapeDtypeStruct(q.shape, BF16), ja...  45.1 us
    unnamed x3, local copies, waits for them, and re-layouts  2.73 us

profile of v3, /device:TPU:25, one launch (start us, length us, event | category | flops | bytes accessed | tf_op | source)
XLA Modules:
  0.0 48.5 jit_solution(10700597276992442221)
XLA Ops:
  0.6 45.1 %shard_map.85 = (bf16[512,2048]{1,0:T(8,128)(2,1)S(1)}, bf16[512,256]{1,0:T(8,128)(2,1)S(1)}, bf16[512,256]{1,0:T(8,128)(2,1)S(1)}) custom-call(bf16[512,2048]{1,0:T(8,128)(2,1)} %q_hbm.1, bf16[512,2048]{1,0:T(8,128)(2,1)} %o_hbm.1, bf16[512,256]{1,0:T(8,128)(2,1)} %k_hbm.1, bf16[512,256]{1,0:T(8,128)(2,1)} %v_hbm.1, s32[1024]{0:T(1024)} %parent_hbm.1, ...), custom_call_target="tpu_custom_call" | custom-call | tf_op jit(solution)/shard_map/pallas_call | solution.py:375
  45.7 1.3 %copy.12 = bf16[512,2048]{1,0:T(8,128)(2,1)} copy(bf16[512,2048]{1,0:T(8,128)(2,1)S(1)} %get-tuple-element.6) | data formatting | bytes 4194304
  47.1 0.7 %copy.13 = bf16[512,256]{1,0:T(8,128)(2,1)} copy(bf16[512,256]{1,0:T(8,128)(2,1)S(1)} %get-tuple-element.7) | data formatting | bytes 524288
  47.8 0.7 %copy.14 = bf16[512,256]{1,0:T(8,128)(2,1)} copy(bf16[512,256]{1,0:T(8,128)(2,1)S(1)} %get-tuple-element.8) | data formatting | bytes 524288

commit v4 on v3

--- a/solution.py
+++ b/solution.py
@@ -368,11 +368,22 @@
                 back(h, part, 2, 0, 1).wait_send()
 
 
+def write_out(dq_in, dk_in, dv_in, dq_out, dk_out, dv_out, sem):
+    copies = [
+        pltpu.make_async_copy(src, dst, sem.at[n])
+        for n, (src, dst) in enumerate(((dq_in, dq_out), (dk_in, dk_out), (dv_in, dv_out)))
+    ]
+    for copy in copies:
+        copy.start()
+    for copy in copies:
+        copy.wait()
+
+
 def shards(q, k, v, o, parent_block, seg_start):
     hbm = pl.BlockSpec(memory_space=pltpu.HBM)
     vmem = pl.BlockSpec(memory_space=pltpu.VMEM)
     width = q.shape[1]
-    return pl.pallas_call(
+    results = pl.pallas_call(
         kernel,
         out_shape=(
             jax.ShapeDtypeStruct(q.shape, BF16),
@@ -406,6 +417,14 @@
             collective_id=0, has_side_effects=True, vmem_limit_bytes=48 * 2**20
         ),
     )(*(pltpu.with_memory_space_constraint(x, pltpu.HBM) for x in (q, o, k, v, parent_block, seg_start)))
+    return pl.pallas_call(
+        write_out,
+        out_shape=tuple(jax.ShapeDtypeStruct(x.shape, x.dtype) for x in results),
+        in_specs=[pl.BlockSpec(memory_space=pl.ANY)] * 3,
+        out_specs=(hbm,) * 3,
+        scratch_shapes=[pltpu.SemaphoreType.DMA((3,))],
+        compiler_params=pltpu.CompilerParams(vmem_limit_bytes=2**20),
+    )(*results)
 
 
 def solution(mesh):

time: 48.5 us -> 47.5 us (0.979)
  local copies, waits for them, and re-layouts: 2.73 us -> 0 us
  Pallas kernels: 45.1 us -> 46.6 us
    unnamed x3 -> x0, local copies, waits for them, and re-layouts: 2.73 us -> none
    pallas_call x0 -> x1, Pallas kernels: none -> 1.51 us  [shards(): pl.pallas_call(write_out, out_shape=tuple((jax.ShapeDtypeStruct(x.shape,...]
where the time goes in v4:
time: 47.5 us; the launch traced here: 47.4 us
  Pallas kernels  46.6 us (98%)
  between operations  0.8 us (2%)
    pallas_call x1, Pallas kernels, shards(): pl.pallas_call(kernel, out_shape=(jax.ShapeDtypeStruct(q.shape, BF16), ja...  45.1 us
    pallas_call x1, Pallas kernels, shards(): pl.pallas_call(write_out, out_shape=tuple((jax.ShapeDtypeStruct(x.shape,...  1.51 us

profile of v4, /device:TPU:25, one launch (start us, length us, event | category | flops | bytes accessed | tf_op | source)
XLA Modules:
  0.0 47.4 jit_solution(15151063653786661067)
XLA Ops:
  0.6 45.1 %shard_map.85 = (bf16[512,2048]{1,0:T(8,128)(2,1)S(1)}, bf16[512,256]{1,0:T(8,128)(2,1)S(1)}, bf16[512,256]{1,0:T(8,128)(2,1)S(1)}) custom-call(bf16[512,2048]{1,0:T(8,128)(2,1)} %q_hbm.1, bf16[512,2048]{1,0:T(8,128)(2,1)} %o_hbm.1, bf16[512,256]{1,0:T(8,128)(2,1)} %k_hbm.1, bf16[512,256]{1,0:T(8,128)(2,1)} %v_hbm.1, s32[1024]{0:T(1024)} %parent_hbm.1, ...), custom_call_target="tpu_custom_call" | custom-call | tf_op jit(solution)/shard_map/pallas_call | solution.py:386
  45.7 1.5 %shard_map.86 = (bf16[512,2048]{1,0:T(8,128)(2,1)}, bf16[512,256]{1,0:T(8,128)(2,1)}, bf16[512,256]{1,0:T(8,128)(2,1)}) custom-call(bf16[512,2048]{1,0:T(8,128)(2,1)S(1)} %get-tuple-element.6.dq_in, bf16[512,256]{1,0:T(8,128)(2,1)S(1)} %get-tuple-element.7.dk_in, bf16[512,256]{1,0:T(8,128)(2,1)S(1)} %get-tuple-element.8.dv_in), custom_call_target="tpu_custom_call" | custom-call | tf_op jit(solution)/shard_map/pallas_call | solution.py:420

commit v5 on v4

--- a/solution.py
+++ b/solution.py
@@ -306,7 +306,6 @@
     send_own(2, near=False)
     relay(1)
     send_own(2, far=False)
-    send_own(3)
     for h in range(HEADS):
         ready(h)
         if h == 2:
@@ -320,23 +319,28 @@
             )
         if h in (1, 2):
             merge_odd(h - 1)
+        if h == 0:
+            send_own(3)
         if h < 2:
             relay(h + 2)
         give(h)
         if h == 2:
             merge_even(1)
+    def finish(h):
+        lanes = slice(64 * h, 64 * h + 128)
+        a, b = own_ref[h], own_ref[h + 1]
+        dk_ref[:, lanes] = jnp.concatenate([a[:, :64], b[:, :64]], 1).astype(BF16)
+        dv_ref[:, lanes] = jnp.concatenate([a[:, 64:], b[:, 64:]], 1).astype(BF16)
+
     merge_odd(3)
     merge_even(2)
     take(0)
     take(1)
     merge_even(3)
+    finish(0)
     take(2)
     take(3)
-    for h in range(0, HEADS, 2):
-        lanes = slice(64 * h, 64 * h + 128)
-        a, b = own_ref[h], own_ref[h + 1]
-        dk_ref[:, lanes] = jnp.concatenate([a[:, :64], b[:, :64]], 1).astype(BF16)
-        dv_ref[:, lanes] = jnp.concatenate([a[:, 64:], b[:, 64:]], 1).astype(BF16)
+    finish(2)
     for h in range(HEADS):
         for part in range(FWD_PARTS[h]):
             @pl.when(even | later)

time: 47.5 us -> 47 us (0.989)
  Pallas kernels: 46.6 us -> 46.1 us
    pallas_call x1, Pallas kernels: 45.1 us -> 44.6 us  [shards(): pl.pallas_call(kernel, out_shape=(jax.ShapeDtypeStruct(q.shape, BF16), ja...]
where the time goes in v5:
time: 47 us; the launch traced here: 46.9 us
  Pallas kernels  46.1 us (98%)
  between operations  0.8 us (2%)
    pallas_call x1, Pallas kernels, shards(): pl.pallas_call(kernel, out_shape=(jax.ShapeDtypeStruct(q.shape, BF16), ja...  44.6 us
    pallas_call x1, Pallas kernels, shards(): pl.pallas_call(write_out, out_shape=tuple((jax.ShapeDtypeStruct(x.shape,...  1.51 us

profile of v5, /device:TPU:25, one launch (start us, length us, event | category | flops | bytes accessed | tf_op | source)
XLA Modules:
  0.0 46.9 jit_solution(577416273554035947)
XLA Ops:
  0.6 44.6 %shard_map.85 = (bf16[512,2048]{1,0:T(8,128)(2,1)S(1)}, bf16[512,256]{1,0:T(8,128)(2,1)S(1)}, bf16[512,256]{1,0:T(8,128)(2,1)S(1)}) custom-call(bf16[512,2048]{1,0:T(8,128)(2,1)} %q_hbm.1, bf16[512,2048]{1,0:T(8,128)(2,1)} %o_hbm.1, bf16[512,256]{1,0:T(8,128)(2,1)} %k_hbm.1, bf16[512,256]{1,0:T(8,128)(2,1)} %v_hbm.1, s32[1024]{0:T(1024)} %parent_hbm.1, ...), custom_call_target="tpu_custom_call" | custom-call | tf_op jit(solution)/shard_map/pallas_call | solution.py:390
  45.2 1.5 %shard_map.86 = (bf16[512,2048]{1,0:T(8,128)(2,1)}, bf16[512,256]{1,0:T(8,128)(2,1)}, bf16[512,256]{1,0:T(8,128)(2,1)}) custom-call(bf16[512,2048]{1,0:T(8,128)(2,1)S(1)} %get-tuple-element.6.dq_in, bf16[512,256]{1,0:T(8,128)(2,1)S(1)} %get-tuple-element.7.dk_in, bf16[512,256]{1,0:T(8,128)(2,1)S(1)} %get-tuple-element.8.dv_in), custom_call_target="tpu_custom_call" | custom-call | tf_op jit(solution)/shard_map/pallas_call | solution.py:424
